TPU v7x, 128 devices: a whole 4x4x4 slice. The times are simulated.
128 devices in a mesh: seq: 8 (over x, core), dp: 16 (over z, y).
Axes of the slice: x: 4, y: 4, z: 4, core: 2. Of those that a mesh axis runs over, the one named last changes fastest.
Arguments:
- queries: bfloat16 [16, 4096, 2048], P('dp', 'seq'), may hold values from -6 to 6
- keys: bfloat16 [16, 4096, 2048], P('dp', 'seq'), may hold values from -6 to 6
- values: bfloat16 [16, 4096, 2048], P('dp', 'seq'), may hold values from -6 to 6
- out_weight: bfloat16 [2048, 2048], replicated, may hold values from -0.125 to 0.125
- out_grad: bfloat16 [16, 4096, 2048], P('dp', 'seq'), may hold values from -6 to 6
Outputs:
- result: bfloat16 [16, 4096, 2048], P('dp', 'seq')
- grad_queries: bfloat16 [16, 4096, 2048], P('dp', 'seq')
- grad_keys: bfloat16 [16, 4096, 2048], P('dp', 'seq')
- grad_values: bfloat16 [16, 4096, 2048], P('dp', 'seq')
- grad_weight: float32 [2048, 2048], P(('seq', 'dp'))
All inputs are finite; a program needn't handle non-finite values.
Results may differ from a plain program's by a relative error of at most 0.0052.
Values sent between devices are 32-bit elements; how exact they have to be, the bound alone decides.
A program may use at most 192 MiB of HBM per device.

v0:
```python
import functools

import jax
import jax.numpy as jnp
from jax import lax
from jax.experimental import pallas as pl
from jax.experimental.pallas import tpu as pltpu
from jax.sharding import PartitionSpec as P

MESH = pl.DeviceIdType.MESH
HEADS = 16
HALF = 8
DH = 128
TOK = 512
MID = 256
HD = 2048
TILES = 8
WIDE = 256
LAG = 2
Y_FIRST, Z_FIRST, X_FIRST = ("y", "z", "x"), ("z", "x", "y"), ("x", "y", "z")
ORDERS = (Y_FIRST, Z_FIRST, X_FIRST)
ALL = slice(None)
A, B = pl.ds(0, MID), pl.ds(MID, MID)
f32, bf16 = jnp.float32, jnp.bfloat16


def place():
    s, d = lax.axis_index("seq"), lax.axis_index("dp")
    return {"x": s // 2, "c": s % 2, "z": d // 4, "y": d % 4}


def device(spot, **moves):
    spot = dict(spot)
    for axis, by in moves.items():
        spot[axis] = (spot[axis] + by) % (2 if axis == "c" else 4)
    return (spot["x"] * 2 + spot["c"], spot["z"] * 4 + spot["y"])


def greet(spot):
    barrier = pltpu.get_barrier_semaphore()
    partners = [device(spot, c=1)]
    for axis in "xyz":
        partners += [device(spot, **{axis: by}) for by in (1, 2, 3)]
    for partner in partners:
        pl.semaphore_signal(barrier, 1, device_id=partner, device_id_type=MESH)
    return lambda: pl.semaphore_wait(barrier, len(partners))


def dot(a, b):
    return jnp.dot(a, b, preferred_element_type=f32)


def dot_nt(a, b):
    return lax.dot_general(a, b, (((1,), (1,)), ((), ())), preferred_element_type=f32)


def lanes(h, size=DH):
    return pl.ds(h * size if isinstance(h, int) else pl.multiple_of(h * size, size), size)


def two(value):
    high = value.astype(bf16)
    return high, (value - high.astype(f32)).astype(bf16)


class Flow:
    def __init__(self, spot, refs, backward):
        self.local, self.pair_in, self.chain_in, self.chain_out, self.share_out, self.state, self.send, self.recv = refs
        self.spot, self.c = spot, spot["c"]
        self.rank = 3 - spot["x"] if backward else spot["x"]
        self.move = 3 if backward else 1
        self.first = (self.c == (1 if backward else 0)).astype(f32)

    @staticmethod
    def scratch():
        full, half = pltpu.VMEM((HEADS, DH, DH), f32), pltpu.VMEM((HALF, DH, DH), f32)
        sems = pltpu.SemaphoreType.DMA((3, HALF))
        return [full, half, half, half, half, full, sems, sems]

    def copy(self, kind, i, src, dst, **move):
        return pltpu.make_async_remote_copy(
            src_ref=src, dst_ref=dst, send_sem=self.send.at[kind, i], recv_sem=self.recv.at[kind, i],
            device_id=device(self.spot, **move), device_id_type=MESH)

    def pair(self, i):
        return self.copy(0, i, self.local.at[HALF * (1 - self.c) + i], self.pair_in.at[i], c=1)

    def chain(self, i):
        return self.copy(1, i, self.chain_out.at[i], self.chain_in.at[i], x=self.move)

    def share(self, i):
        return self.copy(2, i, self.share_out.at[i], self.state.at[HALF * self.c + i], c=1)

    def clear(self):
        @pl.when(self.rank == 0)
        def _():
            self.chain_in[...] = jnp.zeros_like(self.chain_in)

    def step(self, i):
        mine = HALF * self.c + i
        self.pair(i).wait_recv()

        @pl.when(self.rank > 0)
        def _():
            self.chain(i).wait_recv()

        @pl.when(self.rank < 3)
        def _():
            self.chain_out[i] = self.chain_in[i] + (self.local[mine] + self.pair_in[i])
            self.chain(i).start()

        self.share_out[i] = self.chain_in[i] + self.first * self.local[mine]
        self.share(i).start()
        self.state[mine] = self.chain_in[i] + (1.0 - self.first) * self.pair_in[i]

    def due(self, p, start=0):
        late = jnp.maximum(p - 3 * self.rank, 0)
        return jnp.where(self.rank == 0, jnp.where(p <= start, 0, HALF), jnp.minimum((2 * late + 2) // 3, HALF))

    def steps(self, p, start=0):
        lax.fori_loop(self.due(p, start), self.due(p + 1, start), lambda i, _: self.step(i), None)

    def drain(self):
        @pl.loop(0, HALF)
        def _(i):
            self.pair(i).wait_send()
            self.share(i).wait_send()

            @pl.when(self.rank < 3)
            def _():
                self.chain(i).wait_send()


class Scatter:
    def __init__(self, spot, lhs, rhs, out, refs, scale):
        (self.own, self.pair_out, self.r1, self.r2, self.s2,
         self.t2, self.send, self.recv) = refs
        self.spot, self.lhs, self.rhs, self.out, self.scale = spot, lhs, rhs, out, scale

    def each(self, t, body):
        kind = jnp.where(t < 6, t % 2, 2)
        for n, axes in enumerate(ORDERS):
            pl.when(kind == n)(functools.partial(body, axes))

    def view(self, t, sel, rows=ALL):
        return self.own.at[t, sel.get("x", ALL), sel.get("z", ALL), sel.get("y", ALL), rows]

    def copy(self, t, n, src, dst, **move):
        return pltpu.make_async_remote_copy(
            src_ref=src, dst_ref=dst, send_sem=self.send.at[t, n], recv_sem=self.recv.at[t, n],
            device_id=device(self.spot, **move), device_id_type=MESH)

    def pair(self, t):
        return self.copy(t, 0, self.pair_out.at[t % 3], self.own.at[t], c=1)

    def parts(self, t, phase, axes):
        axis = axes[phase]
        me = self.spot[axis]
        fixed = {a: self.spot[a] for a in axes[:phase]}
        chunk = lambda by: {**fixed, axis: (me + by) % 4}
        second = (self.r2, self.s2, self.t2)[phase]
        n = 1 + 4 * phase
        mine = self.view(t, chunk(0))
        if phase:
            def copies(i):
                return self.copy(t, n + i, self.view(t, chunk(i + 1)), second.at[t, i], **{axis: i + 1})

            return copies, (None, None, mine), (None, second.at[t])
        rest = [a for a in "xzy" if a != axis][0]
        half = lambda by, k: self.view(t, {**chunk(by), rest: pl.ds(2 * k, 2)})

        def copies(i):
            src = (half(2, 0), half(2, 1), self.view(t, chunk(1)), self.view(t, chunk(3)))[i]
            dst = (self.r1, self.r1, second, second)[i].at[t, i % 2]
            return self.copy(t, n + i, src, dst, **{axis: 1 + 2 * (i % 2)})

        return copies, (half(1, 0), half(3, 1), mine), (self.r1.at[t], second.at[t])

    def partner_tile(self, t):
        pl.when(t >= 3)(lambda: self.pair(t - 3).wait_send())
        c = self.spot["c"]
        for xx in range(4):
            got = dot(self.lhs[xx, 1 - c], self.rhs[:, lanes(t, WIDE)])
            self.pair_out[t % 3, xx] = got.reshape(4, 4, 16, WIDE)
        self.pair(t).start()

    def own_tile(self, t):
        c = self.spot["c"]
        self.pair(t).wait_recv()
        for xx in range(4):
            got = dot(self.lhs[xx, c], self.rhs[:, lanes(t, WIDE)])
            self.own[t, xx] = self.own[t, xx] + got.reshape(4, 4, 16, WIDE)
        self.each(t, functools.partial(self.begin, t, 0))

    def begin(self, t, phase, axes):
        copies, _, _ = self.parts(t, phase, axes)
        for i in (1, 0, 2) if phase else (0, 1):
            copies(i).start()

    def pass_on(self, t):
        def body(axes):
            copies, (after, before, _), (first, _) = self.parts(t, 0, axes)
            copies(0).wait_recv()
            after[...] = after[...] + first[0]
            copies(2).start()
            copies(1).wait_recv()
            before[...] = before[...] + first[1]
            copies(3).start()

        self.each(t, body)

    def finish(self, t, phase):
        def body(axes):
            copies, (_, _, mine), (_, second) = self.parts(t, phase, axes)
            for i in range(3) if phase else (2, 3):
                copies(i).wait_recv()
            total = mine[...] + second[0] + second[1]
            if phase:
                total = total + second[2]
            if phase == 2:
                self.out[:, lanes(t, WIDE)] = total * self.scale
            else:
                mine[...] = total
                self.begin(t, phase + 1, axes)

        self.each(t, body)

    def drain(self):
        @pl.loop(0, TILES)
        def _(t):
            pl.when(t >= TILES - 3)(lambda: self.pair(t).wait_send())

            def body(axes):
                for phase in range(3):
                    for i in range(3 if phase else 4):
                        self.parts(t, phase, axes)[0](i).wait_send()

            self.each(t, body)

    @staticmethod
    def scratch():
        V = pltpu.VMEM
        return [
            V((TILES, 4, 4, 4, 16, WIDE), f32),
            V((3, 4, 4, 4, 16, WIDE), f32),
            V((TILES, 2, 2, 4, 16, WIDE), f32),
            V((TILES, 2, 4, 4, 16, WIDE), f32),
            V((TILES, 3, 4, 16, WIDE), f32),
            V((TILES, 3, 16, WIDE), f32),
            pltpu.SemaphoreType.DMA((TILES, 13)),
            pltpu.SemaphoreType.DMA((TILES, 13)),
        ]


FLOW = len(Flow.scratch())
SCATTER = len(Scatter.scratch())


def layer(scale, q_in, k_in, v_in, w_in, og_in, res_out, gq_out, gk_out, gv_out, gw_out, *refs):
    (q, k, v, og, g, att, gq, att_t, intra, wrow, wcol, col, tri, tri_t, ctri, ctri_t, crow,
     in_sem, row_sem, col_sem, out_sem) = refs[:21]
    pre_refs, suf_refs, sc_refs = refs[21:21 + FLOW], refs[21 + FLOW:21 + 2 * FLOW], refs[21 + 2 * FLOW:]
    spot = place()
    met = greet(spot)
    c = spot["c"]
    pre, suf = Flow(spot, pre_refs, False), Flow(spot, suf_refs, True)
    scatter = Scatter(spot, att_t, og, gw_out, sc_refs, scale)

    def load(n, src, dst, part):
        cols = pl.ds(pl.multiple_of(part * 1024, 1024), 1024)
        return pltpu.make_async_copy(src.at[:, cols], dst.at[:, cols], in_sem.at[n])

    theirs, ours = 1 - c, c
    loads = {}
    for n, (name, src, dst, part) in enumerate((
            ("k0", k_in, k, theirs), ("v0", v_in, v, theirs), ("k1", k_in, k, ours), ("v1", v_in, v, ours),
            ("q0", q_in, q, theirs), ("q1", q_in, q, ours), ("og0", og_in, og, theirs), ("og1", og_in, og, ours))):
        loads[name] = load(n, src, dst, part)

    def tile_of(p):
        return (p + 4 * theirs) % 8

    def row_tile(p):
        rows = pl.ds(pl.multiple_of(tile_of(p) * WIDE, WIDE), WIDE)
        return pltpu.make_async_copy(w_in.at[rows], wrow.at[p % 3], row_sem.at[p])

    def col_tile(n):
        return pltpu.make_async_copy(w_in.at[:, lanes(n, WIDE)], wcol.at[n % 2], col_sem.at[n])

    for name in ("k0", "v0", "k1", "v1", "q0", "q1"):
        loads[name].start()
    row_tile(0).start()
    loads["og0"].start()
    loads["og1"].start()
    row_tile(1).start()
    row_tile(2).start()

    base = lax.axis_index("seq") * TOK + 1

    def scale_of(shape, dim):
        index = lax.broadcasted_iota(jnp.int32, shape, dim)
        return lax.rsqrt((DH * (index + base)).astype(f32))

    col[...] = scale_of((TOK, DH), 0)
    crow[...] = scale_of((8, TOK), 1)
    below = (lax.broadcasted_iota(jnp.int32, (MID, MID), 0) >= lax.broadcasted_iota(jnp.int32, (MID, MID), 1)).astype(f32)
    above = (lax.broadcasted_iota(jnp.int32, (MID, MID), 0) <= lax.broadcasted_iota(jnp.int32, (MID, MID), 1)).astype(f32)
    tri[...] = below
    for b, rows in enumerate((A, B)):
        ctri[b] = jnp.concatenate([col[rows]] * 2, axis=1) * below
        ctri_t[b] = crow[0:1, rows] * above
    pre.clear()
    suf.clear()
    met()

    def local_state(h):
        pre.local[h] = dot(k[:, lanes(h)].T, v[:, lanes(h)])

    def local_grad(h):
        high, low = two(col[...] * q[:, lanes(h)].astype(f32))
        both = dot(g[:, lanes(h)].T, jnp.concatenate([high, low], axis=1))
        suf.local[h] = both[:, :DH] + both[:, DH:]

    def attend_intra(h):
        hs = lanes(h)
        c_b = jnp.concatenate([col[B]] * 2, axis=1)
        w_a = (dot_nt(q[A, hs], k[A, hs]) * ctri[0]).astype(bf16)
        w_ba = (dot_nt(q[B, hs], k[A, hs]) * c_b).astype(bf16)
        w_bb = (dot_nt(q[B, hs], k[B, hs]) * ctri[1]).astype(bf16)
        intra[h, A] = dot(w_a, v[A, hs])
        intra[h, B] = dot(jnp.concatenate([w_ba, w_bb], axis=1), v[:, hs])

    def attend(h):
        hs = lanes(h)
        high, low = two(pre.state[h])
        x = q[:, hs]
        inter = dot(jnp.concatenate([x, x], axis=1), jnp.concatenate([high, low], axis=0))
        got = (col[...] * inter + intra[h]).astype(bf16)
        att[:, hs] = got
        att_t[h // 4, h % 4 // 2, lanes(h % 2)] = got.T

    def grad_att(p):
        row_tile(p).wait()
        n = tile_of(p)
        g[:, lanes(n, WIDE)] = dot_nt(og[...], wrow[p % 3]).astype(bf16)
        pl.when(p + 3 < TILES)(lambda: row_tile(p + 3).start())

        @pl.loop(0, 2)
        def _(e):
            local_grad(2 * n + e)
            pl.when(p < 4)(lambda: suf.pair(2 * p + e).start())

    def back_q(h):
        hs = lanes(h)
        ga, gb, va, vb = (r[s, hs] for r in (g, v) for s in (A, B))
        gg = g[:, hs]
        r_a = (dot_nt(ga, va) * tri[...]).astype(bf16)
        r_ba = dot_nt(gb, va).astype(bf16)
        r_bb = (dot_nt(gb, vb) * tri[...]).astype(bf16)
        high, low = two(pre.state[h])
        inter = dot_nt(jnp.concatenate([gg, gg], axis=1), jnp.concatenate([high, low], axis=1))
        gq[A, hs] = (col[A] * (inter[:MID] + dot(r_a, k[A, hs]))).astype(bf16)
        gq[B, hs] = (col[B] * (inter[MID:] + dot(jnp.concatenate([r_ba, r_bb], axis=1), k[:, hs]))).astype(bf16)
        head_out(0, h).start()

    def back_kv(h):
        hs = lanes(h)
        ga, gb, va, vb, ka, kb, qa, qb = (r[s, hs] for r in (g, v, k, q) for s in (A, B))
        gg, vv, kk, qq = g[:, hs], v[:, hs], k[:, hs], q[:, hs]
        c_b = crow[0:1, B]
        high, low = two(suf.state[h])
        s_aa = (dot_nt(va, ga) * ctri_t[0]).astype(bf16)
        s_ab = (dot_nt(va, gb) * c_b).astype(bf16)
        s_bb = (dot_nt(vb, gb) * ctri_t[1]).astype(bf16)
        inter = dot(jnp.concatenate([vv, vv], axis=1), jnp.concatenate([high, low], axis=0))
        gk_a = (inter[:MID] + dot(jnp.concatenate([s_aa, s_ab], axis=1), qq)).astype(bf16)
        gk_b = (inter[MID:] + dot(s_bb, qb)).astype(bf16)
        w_aa = (dot_nt(ka, qa) * ctri_t[0]).astype(bf16)
        w_ab = (dot_nt(ka, qb) * c_b).astype(bf16)
        w_bb = (dot_nt(kb, qb) * ctri_t[1]).astype(bf16)
        inter = dot_nt(jnp.concatenate([kk, kk], axis=1), jnp.concatenate([high, low], axis=1))
        gv_a = (inter[:MID] + dot(jnp.concatenate([w_aa, w_ab], axis=1), gg)).astype(bf16)
        gv_b = (inter[MID:] + dot(w_bb, gb)).astype(bf16)
        k[A, hs], k[B, hs] = gk_a, gk_b
        v[A, hs], v[B, hs] = gv_a, gv_b
        for n in (1, 2):
            head_out(n, h).start()

    def head_out(n, h):
        src, dst = ((gq, gq_out), (k, gk_out), (v, gv_out))[n]
        return pltpu.make_async_copy(src.at[:, lanes(h)], dst.at[:, lanes(h)], out_sem.at[n, h])

    def result_out(n):
        return pltpu.make_async_copy(og.at[:, lanes(n, WIDE)], res_out.at[:, lanes(n, WIDE)], out_sem.at[3, n])

    def result(n):
        col_tile(n).wait()
        og[:, lanes(n, WIDE)] = dot(att[...], wcol[n % 2]).astype(bf16)
        result_out(n).start()
        pl.when(n + 2 < TILES)(lambda: col_tile(n + 2).start())

    loads["k0"].wait()
    loads["v0"].wait()
    @pl.loop(0, HALF)
    def _(i):
        local_state(HALF * theirs + i)
        pre.pair(i).start()

    loads["k1"].wait()
    loads["v1"].wait()

    @pl.loop(0, HALF)
    def _(i):
        local_state(HALF * ours + i)
        pl.when(pre.rank == 0)(lambda: pre.step(i))

    for name in ("q0", "q1"):
        loads[name].wait()

    def attend_pair(i, _):
        attend(HALF * c + i)
        pre.share(i).wait_recv()
        attend(HALF * (1 - c) + i)

    def attended(p):
        return jnp.minimum(pre.due(p - 2, -3), jnp.minimum(p // 2, HALF))

    col_tile(0).start()
    col_tile(1).start()
    def attend_due(p):
        lax.fori_loop(attended(p), attended(p + 1), attend_pair, None)

    loads["og0"].wait()
    loads["og1"].wait()

    @pl.loop(0, TILES)
    def _(n):
        pre.steps(2 * n, -1)

        @pl.loop(0, 2)
        def _(e):
            attend_intra(HALF * e + n)

        attend_due(2 * n)
        pre.steps(2 * n + 1, -1)
        grad_att(n)
        attend_due(2 * n + 1)

    suf.steps(0)

    @pl.loop(2 * TILES, 2 * TILES + HALF)
    def _(p):
        pre.steps(p, -1)
        attend_due(p)

        @pl.loop(0, 2)
        def _(e):
            back_q(HALF * ((c + e) % 2) + p - 2 * TILES)

    @pl.loop(0, TILES + 2)
    def _(n):
        pl.when(n < TILES)(lambda: scatter.partner_tile(n))
        pl.when(n >= 2)(lambda: scatter.own_tile(n - 2))
        suf.steps(n + 1)

    @pl.loop(0, TILES)
    def _(n):
        scatter.pass_on(n)
        result(n)
        suf.steps(TILES + 3 + n)

    suf.steps(2 * TILES + 3)
    suf.steps(2 * TILES + 4)

    @pl.loop(0, TILES)
    def _(n):
        scatter.finish(n, 0)

        @pl.loop(0, 2)
        def _(e):
            pl.when(e == 1)(lambda: suf.share(n).wait_recv())
            back_kv(HALF * ((c + e) % 2) + n)

    for phase in (1, 2):
        pl.loop(0, TILES)(lambda n: scatter.finish(n, phase))
    scatter.drain()
    pre.drain()
    suf.drain()
    @pl.loop(0, HEADS)
    def _(h):
        for n in range(3):
            head_out(n, h).wait()

    pl.loop(0, TILES)(lambda n: result_out(n).wait())


def local(queries, keys, values, out_weight, out_grad):
    tokens = lax.axis_size("dp") * lax.axis_size("seq") * TOK
    wide = lambda: pltpu.VMEM((TOK, HD), bf16)
    hbm = pl.BlockSpec(memory_space=pl.ANY)
    rows = jax.ShapeDtypeStruct((TOK, HD), bf16)
    sem = pltpu.SemaphoreType.DMA
    outs = pl.pallas_call(
        functools.partial(layer, float(tokens) ** -0.5),
        out_shape=[rows] * 4 + [jax.ShapeDtypeStruct((16, HD), f32)],
        in_specs=[hbm] * 5,
        out_specs=[hbm] * 4 + [pl.BlockSpec(memory_space=pltpu.VMEM)],
        scratch_shapes=[
            wide(), wide(), wide(), wide(), wide(), wide(), wide(),
            pltpu.VMEM((4, 2, 256, TOK), bf16),
            pltpu.VMEM((HEADS, TOK, DH), f32),
            pltpu.VMEM((3, WIDE, HD), bf16),
            pltpu.VMEM((2, HD, WIDE), bf16),
            pltpu.VMEM((TOK, DH), f32),
            pltpu.VMEM((MID, MID), f32),
            pltpu.VMEM((MID, MID), f32),
            pltpu.VMEM((2, MID, MID), f32),
            pltpu.VMEM((2, MID, MID), f32),
            pltpu.VMEM((8, TOK), f32),
            sem((8,)), sem((TILES,)), sem((TILES,)), sem((4, HEADS)),
        ] + Flow.scratch() + Flow.scratch() + Scatter.scratch(),
        compiler_params=pltpu.CompilerParams(collective_id=0, has_side_effects=True, vmem_limit_bytes=60 * 2**20),
        cost_estimate=pl.CostEstimate(flops=23 * 10**9, bytes_accessed=25 * 10**6, transcendentals=0),
    )(*(x.reshape(TOK, HD) for x in (queries, keys, values)), out_weight, out_grad.reshape(TOK, HD))
    return tuple(x if x.shape[0] == 16 else x.reshape(1, TOK, HD) for x in put(outs))


def put_kernel(*refs):
    ins, outs, held, sem = refs[:5], refs[5:10], refs[10:15], refs[15]
    parts = []
    for n in range(5):
        step = ins[n].shape[0] // 2
        for part in range(2):
            rows = pl.ds(part * step, step)
            parts.append((
                pltpu.make_async_copy(ins[n].at[rows], held[n].at[rows], sem.at[0, n, part]),
                pltpu.make_async_copy(held[n].at[rows], outs[n].at[rows], sem.at[1, n, part])))
    for get, _ in parts:
        get.start()
    for get, give in parts:
        get.wait()
        give.start()
    for _, give in parts:
        give.wait()


def put(arrays):
    hbm = pl.BlockSpec(memory_space=pl.ANY)
    return pl.pallas_call(
        put_kernel,
        out_shape=[jax.ShapeDtypeStruct(x.shape, x.dtype) for x in arrays],
        in_specs=[hbm] * 5,
        out_specs=[hbm] * 5,
        scratch_shapes=[pltpu.VMEM(x.shape, x.dtype) for x in arrays] + [pltpu.SemaphoreType.DMA((2, 5, 2))],
        compiler_params=pltpu.CompilerParams(vmem_limit_bytes=60 * 2**20),
    )(*arrays)


def solution(mesh):
    in_specs = (
        P("dp", "seq", None),
        P("dp", "seq", None),
        P("dp", "seq", None),
        P(),
        P("dp", "seq", None),
    )
    out_specs = (
        P("dp", "seq", None),
        P("dp", "seq", None),
        P("dp", "seq", None),
        P("dp", "seq", None),
        P(("seq", "dp"), None),
    )
    return jax.shard_map(local, mesh=mesh, in_specs=in_specs, out_specs=out_specs, check_vma=False)
```

profile of v0, /device:TPU:0, one launch (start us, length us, event | category | flops | bytes accessed | tf_op | source)
XLA Modules:
  0.0 107.6 jit_solution(4168042279545383520)
XLA Ops:
  0.6 100.5 %shard_map.92 = (bf16[512,2048]{1,0:T(8,128)(2,1)}, bf16[512,2048]{1,0:T(8,128)(2,1)}, bf16[512,2048]{1,0:T(8,128)(2,1)}, bf16[512,2048]{1,0:T(8,128)(2,1)}, f32[16,2048]{1,0:T(8,128)}) custom-call(bf16[512,2048]{1,0:T(8,128)(2,1)} %bitcast.8, bf16[512,2048]{1,0:T(8,128)(2,1)} %bitcast.9, bf16[512,2048]{1,0:T(8,128)(2,1)} %bitcast.10, ...), custom_call_target="tpu_custom_call" | custom-call | flops 23000000512 | bytes 25000000 | tf_op jit(solution)/shard_map/pallas_call | solution.py:503
  101.1 6.5 %shard_map.93 = (bf16[512,2048]{1,0:T(8,128)(2,1)}, bf16[512,2048]{1,0:T(8,128)(2,1)}, bf16[512,2048]{1,0:T(8,128)(2,1)}, bf16[512,2048]{1,0:T(8,128)(2,1)}, f32[16,2048]{1,0:T(8,128)}) custom-call(bf16[512,2048]{1,0:T(8,128)(2,1)} %get-tuple-element.15.refs_0_, bf16[512,2048]{1,0:T(8,128)(2,1)} %get-tuple-element.16.refs_1_, ...), custom_call_target="tpu_custom_call" | custom-call | tf_op jit(solution)/shard_map/pallas_call | solution.py:549
where the time goes:
time: 108 us
  Pallas kernels  107 us (99%)
    pallas_call x1, Pallas kernels, local(): pl.pallas_call(functools.partial(layer, float(tokens) ** (-0.5)), out_sha...  100 us
    pallas_call x1, Pallas kernels, put(): pl.pallas_call(put_kernel, out_shape=[jax.ShapeDtypeStruct(x.shape, x.dty...  6.49 us

commit v1 on v0

--- a/solution.py
+++ b/solution.py
@@ -117,8 +117,8 @@
         late = jnp.maximum(p - 3 * self.rank, 0)
         return jnp.where(self.rank == 0, jnp.where(p <= start, 0, HALF), jnp.minimum((2 * late + 2) // 3, HALF))
 
-    def steps(self, p, start=0):
-        lax.fori_loop(self.due(p, start), self.due(p + 1, start), lambda i, _: self.step(i), None)
+    def steps(self, p, start=0, slots=1):
+        lax.fori_loop(self.due(p, start), self.due(p + slots, start), lambda i, _: self.step(i), None)
 
     def drain(self):
         @pl.loop(0, HALF)
@@ -452,25 +452,19 @@
     def _(p):
         pre.steps(p, -1)
         attend_due(p)
-
-        @pl.loop(0, 2)
-        def _(e):
-            back_q(HALF * ((c + e) % 2) + p - 2 * TILES)
+        pl.when(p % 2 == 1)(lambda: suf.steps((p - 15) // 2))
 
     @pl.loop(0, TILES + 2)
     def _(n):
         pl.when(n < TILES)(lambda: scatter.partner_tile(n))
         pl.when(n >= 2)(lambda: scatter.own_tile(n - 2))
-        suf.steps(n + 1)
+        first = 5 + 16 * n // 10
+        suf.steps(first, slots=5 + 16 * (n + 1) // 10 - first)
 
     @pl.loop(0, TILES)
     def _(n):
         scatter.pass_on(n)
         result(n)
-        suf.steps(TILES + 3 + n)
-
-    suf.steps(2 * TILES + 3)
-    suf.steps(2 * TILES + 4)
 
     @pl.loop(0, TILES)
     def _(n):
@@ -479,6 +473,7 @@
         @pl.loop(0, 2)
         def _(e):
             pl.when(e == 1)(lambda: suf.share(n).wait_recv())
+            back_q(HALF * ((c + e) % 2) + n)
             back_kv(HALF * ((c + e) % 2) + n)
 
     for phase in (1, 2):

time: 108 us -> 102 us (0.944)
  Pallas kernels: 107 us -> 101 us
    pallas_call x1, Pallas kernels: 100 us -> 94.9 us  [local(): pl.pallas_call(functools.partial(layer, float(tokens) ** (-0.5)), out_sha...]
where the time goes in v1:
time: 102 us
  Pallas kernels  101 us (99%)
    pallas_call x1, Pallas kernels, local(): pl.pallas_call(functools.partial(layer, float(tokens) ** (-0.5)), out_sha...  94.9 us
    pallas_call x1, Pallas kernels, put(): pl.pallas_call(put_kernel, out_shape=[jax.ShapeDtypeStruct(x.shape, x.dty...  6.49 us

profile of v1, /device:TPU:0, one launch (start us, length us, event | category | flops | bytes accessed | tf_op | source)
XLA Modules:
  0.0 102.1 jit_solution(11122501200441194332)
XLA Ops:
  0.6 94.9 %shard_map.92 = (bf16[512,2048]{1,0:T(8,128)(2,1)}, bf16[512,2048]{1,0:T(8,128)(2,1)}, bf16[512,2048]{1,0:T(8,128)(2,1)}, bf16[512,2048]{1,0:T(8,128)(2,1)}, f32[16,2048]{1,0:T(8,128)}) custom-call(bf16[512,2048]{1,0:T(8,128)(2,1)} %bitcast.8, bf16[512,2048]{1,0:T(8,128)(2,1)} %bitcast.9, bf16[512,2048]{1,0:T(8,128)(2,1)} %bitcast.10, ...), custom_call_target="tpu_custom_call" | custom-call | flops 23000000512 | bytes 25000000 | tf_op jit(solution)/shard_map/pallas_call | solution.py:498
  95.6 6.5 %shard_map.93 = (bf16[512,2048]{1,0:T(8,128)(2,1)}, bf16[512,2048]{1,0:T(8,128)(2,1)}, bf16[512,2048]{1,0:T(8,128)(2,1)}, bf16[512,2048]{1,0:T(8,128)(2,1)}, f32[16,2048]{1,0:T(8,128)}) custom-call(bf16[512,2048]{1,0:T(8,128)(2,1)} %get-tuple-element.15.refs_0_, bf16[512,2048]{1,0:T(8,128)(2,1)} %get-tuple-element.16.refs_1_, ...), custom_call_target="tpu_custom_call" | custom-call | tf_op jit(solution)/shard_map/pallas_call | solution.py:544

commit v2 on v1

--- a/solution.py
+++ b/solution.py
@@ -454,17 +454,18 @@
         attend_due(p)
         pl.when(p % 2 == 1)(lambda: suf.steps((p - 15) // 2))
 
-    @pl.loop(0, TILES + 2)
+    @pl.loop(0, TILES + 6)
     def _(n):
         pl.when(n < TILES)(lambda: scatter.partner_tile(n))
-        pl.when(n >= 2)(lambda: scatter.own_tile(n - 2))
+        pl.when(jnp.logical_and(n >= 2, n < TILES + 2))(lambda: scatter.own_tile(n - 2))
+        pl.when(n >= 6)(lambda: scatter.pass_on(n - 6))
         first = 5 + 16 * n // 10
         suf.steps(first, slots=5 + 16 * (n + 1) // 10 - first)
 
-    @pl.loop(0, TILES)
-    def _(n):
-        scatter.pass_on(n)
-        result(n)
+        @pl.when(n >= TILES + 2)
+        def _():
+            pl.loop(0, 2)(lambda e: result(2 * (n - TILES - 2) + e))
+
 
     @pl.loop(0, TILES)
     def _(n):

time: 102 us -> 101 us (level)
  Pallas kernels: 101 us -> 99.9 us
    pallas_call x1, Pallas kernels: 94.9 us -> 93.5 us  [local(): pl.pallas_call(functools.partial(layer, float(tokens) ** (-0.5)), out_sha...]
where the time goes in v2:
time: 101 us
  Pallas kernels  99.9 us (99%)
    pallas_call x1, Pallas kernels, local(): pl.pallas_call(functools.partial(layer, float(tokens) ** (-0.5)), out_sha...  93.5 us
    pallas_call x1, Pallas kernels, put(): pl.pallas_call(put_kernel, out_shape=[jax.ShapeDtypeStruct(x.shape, x.dty...  6.49 us

profile of v2, /device:TPU:0, one launch (start us, length us, event | category | flops | bytes accessed | tf_op | source)
XLA Modules:
  0.0 100.6 jit_solution(16489954211446456566)
XLA Ops:
  0.6 93.5 %shard_map.92 = (bf16[512,2048]{1,0:T(8,128)(2,1)}, bf16[512,2048]{1,0:T(8,128)(2,1)}, bf16[512,2048]{1,0:T(8,128)(2,1)}, bf16[512,2048]{1,0:T(8,128)(2,1)}, f32[16,2048]{1,0:T(8,128)}) custom-call(bf16[512,2048]{1,0:T(8,128)(2,1)} %bitcast.8, bf16[512,2048]{1,0:T(8,128)(2,1)} %bitcast.9, bf16[512,2048]{1,0:T(8,128)(2,1)} %bitcast.10, ...), custom_call_target="tpu_custom_call" | custom-call | flops 23000000512 | bytes 25000000 | tf_op jit(solution)/shard_map/pallas_call | solution.py:499
  94.1 6.5 %shard_map.93 = (bf16[512,2048]{1,0:T(8,128)(2,1)}, bf16[512,2048]{1,0:T(8,128)(2,1)}, bf16[512,2048]{1,0:T(8,128)(2,1)}, bf16[512,2048]{1,0:T(8,128)(2,1)}, f32[16,2048]{1,0:T(8,128)}) custom-call(bf16[512,2048]{1,0:T(8,128)(2,1)} %get-tuple-element.15.refs_0_, bf16[512,2048]{1,0:T(8,128)(2,1)} %get-tuple-element.16.refs_1_, ...), custom_call_target="tpu_custom_call" | custom-call | tf_op jit(solution)/shard_map/pallas_call | solution.py:545
